TPU v7x, 256 devices: a whole 4x4x8 slice. The times are simulated.
256 devices in a mesh: row: 16 (over y_lo, z), col: 16 (over x, y_hi, core).
Axes of the slice: x: 4, y: 4 (y_hi: 2, y_lo: 2; y = y_hi * 2 + y_lo), z: 8, core: 2. Of those that a mesh axis runs over, the one named last changes fastest.
Arguments:
- pair_act: bfloat16 [512, 512, 128], P('row', 'col'), may hold values from -6 to 6
- residue_mask: int32 [512], replicated, may hold values 0 or 1
- outgoing_weights: bfloat16 [128, 640], replicated, may hold values from -0.5 to 0.5
- outgoing_final: bfloat16 [128, 128], replicated, may hold values from -0.5 to 0.5
- incoming_weights: bfloat16 [128, 640], replicated, may hold values from -0.5 to 0.5
- incoming_final: bfloat16 [128, 128], replicated, may hold values from -0.5 to 0.5
Outputs:
- pair_out: bfloat16 [512, 512, 128], P('row', 'col')
All inputs are finite; a program needn't handle non-finite values.
Results may differ from a plain program's by a relative error of at most 0.015.
Values may be sent and summed in bfloat16 or wider, within the bound.
A program may use at most 128 MiB of HBM per device.

v0:
```python
import jax
import jax.numpy as jnp
from jax import lax
from jax.sharding import PartitionSpec as P


def layer_norm(values):
    middle = jnp.mean(values, axis=-1, keepdims=True)
    centred = values - middle
    spread = jnp.mean(centred * centred, axis=-1, keepdims=True)
    return centred * lax.rsqrt(spread + 1e-05)


def project(pair_act, valid_rows, valid_cols, weights):
    rows_here, cols_here, channels = pair_act.shape
    hidden_width = (weights.shape[1] - channels) // 4
    normed = layer_norm(pair_act.astype(jnp.float32)).astype(jnp.bfloat16)
    pair_mask = (valid_rows[:, None] * valid_cols[None, :])[..., None]
    mixed = jnp.dot(normed.reshape(-1, channels), weights, preferred_element_type=jnp.float32)
    mixed = mixed.reshape(rows_here, cols_here, weights.shape[1])
    left = (
        pair_mask
        * jax.nn.sigmoid(mixed[..., hidden_width : 2 * hidden_width])
        * mixed[..., :hidden_width]
    ).astype(jnp.bfloat16)
    right = (
        pair_mask
        * jax.nn.sigmoid(mixed[..., 3 * hidden_width : 4 * hidden_width])
        * mixed[..., 2 * hidden_width : 3 * hidden_width]
    ).astype(jnp.bfloat16)
    gate_values = jax.nn.sigmoid(mixed[..., 4 * hidden_width :])
    return (left, right, gate_values)


def finish(summed, pair_act, gate_values, final):
    rows_here, cols_here, channels = pair_act.shape
    hidden = layer_norm(summed).astype(jnp.bfloat16)
    update = jnp.dot(hidden.reshape(-1, final.shape[0]), final, preferred_element_type=jnp.float32)
    update = update.reshape(rows_here, cols_here, channels)
    return (pair_act.astype(jnp.float32) + gate_values * update).astype(jnp.bfloat16)


def share_right(right):
    return lax.all_gather(right, "row", axis=0, tiled=True)


def shards(
    pair_act, residue_mask, outgoing_weights, outgoing_final, incoming_weights, incoming_final
):
    rowband = pair_act.shape[0]
    colband = pair_act.shape[1]
    row_index = lax.axis_index("row")
    col_index = lax.axis_index("col")
    valid = residue_mask.astype(jnp.float32)
    valid_rows = lax.dynamic_slice_in_dim(valid, row_index * rowband, rowband, 0)
    valid_cols = lax.dynamic_slice_in_dim(valid, col_index * colband, colband, 0)
    left, right, gate_values = project(pair_act, valid_rows, valid_cols, outgoing_weights)
    right_whole = share_right(right)
    left_rows = lax.all_gather(left, "col", axis=1, tiled=True)
    right_turned = lax.all_to_all(right_whole, "col", split_axis=0, concat_axis=1, tiled=True)
    summed = jnp.einsum("ikh,jkh->ijh", left_rows, right_turned, preferred_element_type=jnp.float32)
    middle_pair = finish(summed, pair_act, gate_values, outgoing_final)
    left, right, gate_values = project(middle_pair, valid_rows, valid_cols, incoming_weights)
    left_whole = lax.all_gather(left, "col", axis=1, tiled=True)
    right_cols = lax.all_gather(right, "row", axis=0, tiled=True)
    left_turned = lax.all_to_all(left_whole, "row", split_axis=1, concat_axis=0, tiled=True)
    summed = jnp.einsum("kih,kjh->ijh", left_turned, right_cols, preferred_element_type=jnp.float32)
    return finish(summed, middle_pair, gate_values, incoming_final)


def solution(mesh):
    return jax.shard_map(
        shards,
        mesh=mesh,
        in_specs=(P("row", "col", None), P(), P(), P(), P(), P()),
        out_specs=P("row", "col", None),
        check_vma=False,
    )
```

profile of v0, /device:TPU:1, one launch (start us, length us, event | category | flops | bytes accessed | tf_op | source)
XLA Modules:
  0.0 474.8 jit_solution(14658494591704481962)
XLA Ops:
  6.5 0.7 convert_element_type.43
  7.3 1.2 convert_reduce_fusion
  8.4 1.3 fusion.7
  9.8 0.1 fusion.46
  9.9 0.1 broadcast_multiply_fusion
  9.9 1.6 fusion.36
  11.5 1.5 copy-done.2
  13.0 1.1 fusion.22
  14.1 0.0 all-gather.7.cloned.1.call-start
  14.2 0.7 all-gather.7.cloned.1.call-update
  14.9 71.2 %all-gather.5.cloned.1.call-done = bf16[512,32,128]{2,1,0:T(8,128)(2,1)} async-done(((bf16[32,32,128]{2,1,0:T(8,128)(2,1)}), bf16[512,32,128]{2,1,0:T(8,128)(2,1)}) %all-gather.5.cloned.1.call-update) | async-done | bytes 4194320 | tf_op jit(solution)/shard_map/all_gather | solution.py:44
  86.1 15.9 %all-to-all-start = ((bf16[512,32,128]{2,1,0:T(8,128)(2,1)}), bf16[512,32,128]{2,1,0:T(8,128)(2,1)}, u32[]{:S(2)}, u32[]{:S(2)}) async-start(bf16[512,32,128]{2,1,0:T(8,128)(2,1)} %all-gather.5.cloned.1.call-done), calls=%async_computation | async-start | bytes 8388608 | tf_op jit(solution)/shard_map/all_to_all | solution.py:60
  102.1 82.7 %all-gather.7.cloned.1.call-done = bf16[32,512,128]{2,1,0:T(8,128)(2,1)} async-done(((bf16[32,32,128]{2,1,0:T(8,128)(2,1)}), bf16[32,512,128]{2,1,0:T(8,128)(2,1)}) %all-gather.7.cloned.1.call-update) | async-done | bytes 4194320 | tf_op jit(solution)/shard_map/all_gather | solution.py:59
  184.8 7.9 %copy.56 = bf16[32,512,128]{1,0,2:T(8,128)(2,1)} copy(bf16[32,512,128]{2,1,0:T(8,128)(2,1)} %all-gather.7.cloned.1.call-done) | data formatting | bytes 8388608 | tf_op jit(solution)/shard_map/all_gather | solution.py:59
  192.8 5.5 %copy.54 = bf16[32,16,32,128]{3,2,1,0:T(8,128)(2,1)} copy(bf16[32,16,32,128]{3,2,0,1:T(8,128)(2,1)} %bitcast.2) | data formatting | bytes 8388608 | tf_op jit(solution)/shard_map/all_to_all | solution.py:60
  198.3 7.9 %copy.55 = bf16[32,512,128]{1,0,2:T(8,128)(2,1)} copy(bf16[32,512,128]{2,1,0:T(8,128)(2,1)} %bitcast.42) | data formatting | bytes 8388608 | tf_op jit(solution)/shard_map/all_to_all | solution.py:60
  206.2 4.7 bitcast_reduce_fusion.1
  210.9 0.1 copy.57
  211.0 0.1 copy.58
  211.1 0.3 multiply_reduce_fusion.1
  211.4 0.1 copy.59
  211.5 0.1 copy.60
  211.6 0.3 multiply_convert_fusion.1
  211.9 1.3 copy.61
  213.2 1.5 fusion.47
  214.7 0.4 multiply_reduce_fusion.2
  215.1 0.4 copy-done.4
  215.5 0.6 fusion.35
  216.1 1.5 copy-done.3
  217.6 1.1 fusion.9
  218.8 0.0 all-gather.9.cloned.1.call-start
  218.8 0.5 all-gather.9.cloned.1.call-update
  219.3 66.4 %all-gather.11.cloned.1.call-done = bf16[32,512,128]{2,1,0:T(8,128)(2,1)} async-done(((bf16[32,32,128]{2,1,0:T(8,128)(2,1)}), bf16[32,512,128]{2,1,0:T(8,128)(2,1)}) %all-gather.11.cloned.1.call-update) | async-done | bytes 4194320 | tf_op jit(solution)/shard_map/all_gather | solution.py:64
  285.8 6.8 %copy.62 = bf16[32,512,128]{2,0,1:T(8,128)(2,1)} copy(bf16[32,512,128]{2,1,0:T(8,128)(2,1)} %all-gather.11.cloned.1.call-done) | data formatting | bytes 8388608 | tf_op jit(solution)/shard_map/all_gather | solution.py:64
  292.6 6.9 %all-to-all-start.1 = ((bf16[32,512,128]{2,0,1:T(8,128)(2,1)}), bf16[32,512,128]{2,0,1:T(8,128)(2,1)}, u32[]{:S(2)}, u32[]{:S(2)}) async-start(bf16[32,512,128]{2,0,1:T(8,128)(2,1)} %copy.62), calls=%async_computation.1 | async-start | bytes 8388608 | tf_op jit(solution)/shard_map/all_to_all | solution.py:66
  299.6 136.5 %all-gather.9.cloned.1.call-done = bf16[512,32,128]{2,1,0:T(8,128)(2,1)} async-done(((bf16[32,32,128]{2,1,0:T(8,128)(2,1)}), bf16[512,32,128]{2,1,0:T(8,128)(2,1)}) %all-gather.9.cloned.1.call-update) | async-done | bytes 4194320 | tf_op jit(solution)/shard_map/all_gather | solution.py:65
  436.0 8.6 %copy.65 = bf16[512,32,128]{0,1,2:T(8,128)(2,1)} copy(bf16[512,32,128]{2,1,0:T(8,128)(2,1)} %all-gather.9.cloned.1.call-done) | data formatting | bytes 8388608 | tf_op jit(solution)/shard_map/all_gather | solution.py:65
  444.6 6.0 %copy.64 = bf16[16,32,32,128]{3,2,1,0:T(8,128)(2,1)} copy(bf16[16,32,32,128]{3,1,2,0:T(8,128)(2,1)} %bitcast.9) | data formatting | bytes 8388608 | tf_op jit(solution)/shard_map/all_to_all | solution.py:66
  450.6 8.6 %copy.66 = bf16[512,32,128]{0,1,2:T(8,128)(2,1)} copy(bf16[512,32,128]{2,1,0:T(8,128)(2,1)} %bitcast.43) | data formatting | bytes 8388608 | tf_op jit(solution)/shard_map/all_to_all | solution.py:66
  459.2 4.7 bitcast_reduce_fusion
  463.9 0.1 copy.67
  463.9 0.1 copy.68
  464.0 0.3 multiply_reduce_fusion
  464.4 0.1 copy.69
  464.5 0.1 copy.70
  464.5 0.3 multiply_convert_fusion
  464.8 1.3 copy.71
  466.1 2.1 fusion.2
  (27 shorter events, 0.2 us)
Async XLA Ops:
  6.5 3.4 copy-start
  6.5 79.6 %all-gather.5.cloned.1.call-start = ((), (), s32[]{:S(2)}) async-start(), calls=%async_computation.2 | async-start | bytes 4456448 | tf_op jit(solution)/shard_map/all_gather | solution.py:44
  11.5 1.5 copy-start.2
  14.1 170.7 %all-gather.7.cloned.1.call-start = ((), (), s32[]{:S(2)}) async-start(), calls=%async_computation.3 | async-start | bytes 4456448 | tf_op jit(solution)/shard_map/all_gather | solution.py:59
  86.1 106.6 %all-to-all-start = ((bf16[512,32,128]{2,1,0:T(8,128)(2,1)}), bf16[512,32,128]{2,1,0:T(8,128)(2,1)}, u32[]{:S(2)}, u32[]{:S(2)}) async-start(bf16[512,32,128]{2,1,0:T(8,128)(2,1)} %all-gather.5.cloned.1.call-done), calls=%async_computation | async-start | bytes 8388608 | tf_op jit(solution)/shard_map/all_to_all | solution.py:60
  102.1 183.7 %all-gather.11.cloned.1.call-start = ((), (), s32[]{:S(2)}) async-start(), calls=%async_computation.5 | async-start | bytes 4456448 | tf_op jit(solution)/shard_map/all_gather | solution.py:64
  211.4 1.8 copy-start.6
  211.9 3.6 copy-start.5
  214.7 0.8 copy-start.4
  216.1 1.5 copy-start.3
  218.8 217.3 %all-gather.9.cloned.1.call-start = ((), (), s32[]{:S(2)}) async-start(), calls=%async_computation.4 | async-start | bytes 4456448 | tf_op jit(solution)/shard_map/all_gather | solution.py:65
  292.6 152.0 %all-to-all-start.1 = ((bf16[32,512,128]{2,0,1:T(8,128)(2,1)}), bf16[32,512,128]{2,0,1:T(8,128)(2,1)}, u32[]{:S(2)}, u32[]{:S(2)}) async-start(bf16[32,512,128]{2,0,1:T(8,128)(2,1)} %copy.62), calls=%async_computation.1 | async-start | bytes 8388608 | tf_op jit(solution)/shard_map/all_to_all | solution.py:66
  464.4 1.8 copy-start.7
  464.5 3.8 copy-start.1
Sparse Core Ops, SparseCore 0:
  14.3 71.8 all-gather.4
  88.7 96.0 all-gather.6
  218.9 66.8 all-gather.10
  287.4 148.5 all-gather.8
where the time goes:
time: 478 us; the launch traced here: 475 us
  waiting for transfers between devices  358 us (75%)
  local copies, waits for them, and re-layouts  58.1 us (12%)
  starting transfers between devices  22.9 us (5%)
  matrix products  15.2 us (3%)
  between operations  13.3 us (3%)
  other arithmetic  7.14 us (1%)
    all_gather x1, waiting for transfers between devices, shards(): right_cols = lax.all_gather(right, 'row', axis=0, tiled=True)  136 us
    all_gather x1, waiting for transfers between devices, shards(): left_rows = lax.all_gather(left, 'col', axis=1, tiled=True)  82.7 us
    all_gather x1, waiting for transfers between devices, share_right(): return lax.all_gather(right, 'row', axis=0, tiled=True)  71.2 us
    all_gather x1, waiting for transfers between devices, shards(): left_whole = lax.all_gather(left, 'col', axis=1, tiled=True)  66.4 us
    all_to_all x1, starting transfers between devices, shards(): lax.all_to_all(right_whole, 'col', split_axis=0, concat_axis=1, tiled=True)  15.9 us
    all_to_all x2, local copies, waits for them, and re-layouts, shards(): lax.all_to_all(left_whole, 'row', split_axis=1, concat_axis=0, tiled=True)  14.6 us
    all_to_all x2, local copies, waits for them, and re-layouts, shards(): lax.all_to_all(right_whole, 'col', split_axis=0, concat_axis=1, tiled=True)  13.5 us
  transfers between devices with their start and end apart: 6, of which 4 were waited for; matrix products, arithmetic and copies ran while one was open for 5% of the time, Pallas kernels for 0%

commit v1 on v0

v1 whole, which is shorter than its diff:
```python
import functools

import jax
import jax.numpy as jnp
from jax import lax
from jax.experimental import pallas as pl
from jax.experimental.pallas import tpu as pltpu
from jax.sharding import PartitionSpec as P

ROWS = 16
COLS = 16
CH = 128
BLK = 32
SUB = 8
CHUNKS = 4
PER = ROWS // CHUNKS


def block_transpose(parts):
    lane = lax.broadcasted_iota(jnp.int32, parts[0].shape, 1)
    low = lane < 64
    even = (lane // 32) % 2 == 0
    t0, t1, t2, t3 = parts
    u0 = jnp.where(low, t0, pltpu.roll(t2, 64, 1))
    u2 = jnp.where(low, pltpu.roll(t0, 64, 1), t2)
    u1 = jnp.where(low, t1, pltpu.roll(t3, 64, 1))
    u3 = jnp.where(low, pltpu.roll(t1, 64, 1), t3)
    return (
        jnp.where(even, u0, pltpu.roll(u1, 32, 1)),
        jnp.where(even, pltpu.roll(u0, 96, 1), u1),
        jnp.where(even, u2, pltpu.roll(u3, 32, 1)),
        jnp.where(even, pltpu.roll(u2, 96, 1), u3),
    )


def kernel(
    mask_ref, pair_ref, w_out, f_out, w_in, f_in, out_ref,
    pair_t, weights_t, final_t, half_mask, normed, mixed, gate, stage,
    send1, recv1, recv2, left_o, left_i, right, summed, send3, recv3, send4, recv4,
    hidden, hidden_t,
    s1, r1, s2, r2, s3, r3, s4, r4,
):
    row, col = lax.axis_index("row"), lax.axis_index("col")
    y_lo, z = row // 8, row % 8
    x, y_hi, core = col // 4, (col // 2) % 2, col % 2
    chip = col // 2

    def z_step(b):
        return ((b + 1) // 2) * (2 * (b % 2) - 1)

    def row_to(d):
        return ((y_lo + d % 2) % 2) * 8 + (z + z_step(d // 2) + 8) % 8

    def row_from(d):
        return ((y_lo + d % 2) % 2) * 8 + (z - z_step(d // 2) + 8) % 8

    def col_to(e):
        return ((x + e // 4) % 4) * 4 + ((y_hi + (e // 2) % 2) % 2) * 2 + (core + e % 2) % 2

    def col_from(e):
        return ((x + 4 - e // 4) % 4) * 4 + ((y_hi + (e // 2) % 2) % 2) * 2 + (core + e % 2) % 2

    barrier = pltpu.get_barrier_semaphore()

    @pl.loop(1, 16)
    def _(d):
        pl.semaphore_signal(barrier, inc=1, device_id={"row": row_to(d)}, device_id_type=pl.DeviceIdType.MESH)
        pl.semaphore_signal(barrier, inc=1, device_id={"col": col_to(d)}, device_id_type=pl.DeviceIdType.MESH)

    for s in range(SUB):
        block = jnp.concatenate([pair_ref[8 * q + s] for q in range(4)], axis=0)
        pair_t[:, s * 128 : (s + 1) * 128] = block.astype(jnp.float32).T
    for u, (w, f) in enumerate(((w_out, f_out), (w_in, f_in))):
        weights_t[u] = w[...].astype(jnp.float32).T.astype(jnp.bfloat16)
        final_t[u] = f[...].astype(jnp.float32).T.astype(jnp.bfloat16)

    lane = lax.broadcasted_iota(jnp.int32, (SUB, 128), 1)
    sub = lax.broadcasted_iota(jnp.int32, (SUB, 128), 0)
    by_row = jnp.zeros((SUB, 128), jnp.float32)
    by_col = jnp.zeros((SUB, 128), jnp.float32)
    for k in range(BLK):
        by_col = jnp.where(lane % 32 == k, mask_ref[col * BLK + k].astype(jnp.float32), by_col)
        by_row = jnp.where(
            (lane // 32) * 8 + sub == k, mask_ref[row * BLK + k].astype(jnp.float32), by_row
        )
    half_mask[...] = 0.5 * by_row * by_col

    def row_copy(src, dst, ssem, rsem, d):
        return pltpu.make_async_remote_copy(
            src_ref=src, dst_ref=dst, send_sem=ssem, recv_sem=rsem,
            device_id={"row": row_to(d)}, device_id_type=pl.DeviceIdType.MESH,
        )

    def col_copy(src, dst, ssem, rsem, e):
        return pltpu.make_async_remote_copy(
            src_ref=src, dst_ref=dst, send_sem=ssem, recv_sem=rsem,
            device_id={"col": col_to(e)}, device_id_type=pl.DeviceIdType.MESH,
        )

    def copy1(u, d):
        return row_copy(send1.at[u, d], recv1.at[u, d], s1.at[u, d], r1.at[u, d], d)

    def copy2(u, g, e):
        there = col_to(e) // 2
        return col_copy(
            recv1.at[u, pl.ds(g * PER, PER), there], recv2.at[u, col, pl.ds(g * PER, PER)],
            s2.at[u, g, e], r2.at[u, g, e], e,
        )

    def copy3(u, e):
        return col_copy(send3.at[u, col_to(e)], recv3.at[u, col], s3.at[u, e], r3.at[u, e], e)

    def copy4(u, d):
        return row_copy(send4.at[u, row_to(d)], recv4.at[u, row], s4.at[u, d], r4.at[u, d], d)

    def project(u):
        for j in range(4):
            cols = slice(256 * j, 256 * (j + 1))
            values = pair_t[:, cols]
            middle = jnp.mean(values, axis=0, keepdims=True)
            centred = values - middle
            spread = jnp.mean(centred * centred, axis=0, keepdims=True)
            normed[:, cols] = (centred * lax.rsqrt(spread + 1e-05)).astype(jnp.bfloat16)
            mixed[:, cols] = jnp.dot(
                weights_t[u], normed[:, cols], preferred_element_type=jnp.float32
            )

    def sides(u, d):
        at = row_to(d) * 8

        def part(k):
            return mixed[pl.ds(pl.multiple_of(at + k * CH, 8), 8), :]

        for side in range(2):
            value, gates = part(2 * side), part(2 * side + 1)
            for s in range(SUB):
                cols = slice(s * 128, (s + 1) * 128)
                stage[pl.ds(side * 8 + s, 8, stride=16), :] = (
                    (jnp.tanh(0.5 * gates[:, cols]) + 1.0) * value[:, cols] * half_mask[s : s + 1, :]
                )
        return stage[...].astype(jnp.bfloat16).reshape(8, 16, 128)

    def assemble_right(u, g):
        for cc in range(4):
            tiles = [
                recv2[u, 4 * cc + t, pl.ds(g * PER, PER)].astype(jnp.float32)[:, 8:].reshape(PER * 8, 128)
                for t in range(4)
            ]
            turned = block_transpose(tiles)
            for i in range(PER):
                rows = jnp.concatenate([v[8 * i : 8 * i + 8] for v in turned], axis=0)
                at = pl.multiple_of(row_from(g * PER + i) * BLK, BLK)
                right[pl.ds(at, BLK), cc * 128 : (cc + 1) * 128] = rows.astype(jnp.bfloat16)

    def assemble_left_o(u, g):
        a = (core + y_lo) % 2
        for cc in range(4):
            tiles = [
                jnp.concatenate(
                    [recv2[u, 4 * cc + t, g * PER + 2 * i + a].astype(jnp.float32)[:8] for i in range(PER // 2)],
                    axis=0,
                )
                for t in range(4)
            ]
            turned = block_transpose(tiles)
            for i in range(PER // 2):
                rows = jnp.concatenate([v[8 * i : 8 * i + 8] for v in turned], axis=0)
                at = pl.multiple_of((row_from(g * PER + 2 * i) % 8) * BLK, BLK)
                left_o[pl.ds(at, BLK), cc * 128 : (cc + 1) * 128] = rows.astype(jnp.bfloat16)

    def assemble_left_i(u, g):
        for cc in range(2):
            tiles = [
                recv2[u, (2 * core + cc) * 4 + t, pl.ds(g * PER, PER)]
                .astype(jnp.float32)[:, :8]
                .reshape(PER * 8, 128)
                for t in range(4)
            ]
            turned = block_transpose(tiles)
            for i in range(PER):
                rows = jnp.concatenate([v[8 * i : 8 * i + 8] for v in turned], axis=0)
                at = pl.multiple_of(row_from(g * PER + i) * BLK, BLK)
                left_i[pl.ds(at, BLK), cc * 128 : (cc + 1) * 128] = rows.astype(jnp.bfloat16)

    for u in range(2):
        project(u)
        if u == 0:
            pl.semaphore_wait(barrier, 30)

        recv1[u, 0] = sides(u, 0)

        @pl.loop(1, ROWS)
        def _(d):
            send1[u, d] = sides(u, d)
            copy1(u, d).start()

        gate[...] = 0.5 * jnp.tanh(0.5 * mixed[4 * CH :, :]) + 0.5

        @pl.loop(0, CHUNKS)
        def _(g):
            @pl.loop(g * PER, (g + 1) * PER)
            def _(d):
                @pl.when(d > 0)
                def _():
                    copy1(u, d).wait_recv()

            @pl.loop(1, COLS)
            def _(e):
                copy2(u, g, e).start()

            recv2[u, col, pl.ds(g * PER, PER)] = recv1[u, pl.ds(g * PER, PER), chip]

        @pl.loop(0, CHUNKS)
        def _(g):
            @pl.loop(1, COLS)
            def _(e):
                copy2(u, g, e).wait_recv()

            assemble_right(u, g)
            if u == 0:
                assemble_left_o(u, g)
            else:
                assemble_left_i(u, g)

        if u == 0:
            summed[...] = lax.dot_general(
                left_o[...], right[...], (((1,), (1,)), ((), ())), preferred_element_type=jnp.float32
            )
        else:
            summed[...] = lax.dot_general(
                left_i[...], right[...], (((0,), (0,)), ((), ())), preferred_element_type=jnp.float32
            )

        for pair in range(4):
            for cc in range(4):
                parts = [
                    jnp.concatenate(
                        [
                            summed[64 * pair + 32 * i + 8 * q : 64 * pair + 32 * i + 8 * q + 8, cc * 128 : (cc + 1) * 128]
                            for i in range(2)
                        ],
                        axis=0,
                    )
                    for q in range(4)
                ]
                for t, tile in enumerate(block_transpose(parts)):
                    send3[u, 4 * cc + t, 16 * pair : 16 * pair + 16, :] = tile.astype(jnp.bfloat16)

        @pl.loop(1, COLS)
        def _(e):
            copy3(u, e).start()

        recv3[u, col] = send3[u, col]

        @pl.loop(1, COLS)
        def _(e):
            copy3(u, e).wait_recv()

        for half in range(2):
            for pair in range(4):
                first = recv3[u, 4 * pair + half].astype(jnp.float32)
                second = recv3[u, 4 * pair + 2 + half].astype(jnp.float32)
                for k in range(8):
                    tile = jnp.concatenate([first[8 * k : 8 * k + 8], second[8 * k : 8 * k + 8]], axis=0)
                    send4[u, 8 * half + k, 16 * pair : 16 * pair + 16, :] = tile.astype(jnp.bfloat16)

        @pl.loop(1, ROWS)
        def _(d):
            copy4(u, d).start()

        recv4[u, row] = send4[u, row]

        @pl.loop(1, ROWS)
        def _(d):
            copy4(u, d).wait_recv()

        total = jnp.zeros((SUB, 128), jnp.float32)
        for k in range(ROWS):
            total += jnp.sum(recv4[u, k].astype(jnp.float32).reshape(8, SUB, 128), axis=0)
        middle = total * (1.0 / CH)
        total = jnp.zeros((SUB, 128), jnp.float32)
        for k in range(ROWS):
            centred = recv4[u, k].astype(jnp.float32).reshape(8, SUB, 128) - middle
            total += jnp.sum(centred * centred, axis=0)
        scale = lax.rsqrt(total * (1.0 / CH) + 1e-05)
        for k in range(ROWS):
            centred = recv4[u, k].astype(jnp.float32).reshape(8, SUB, 128) - middle
            hidden[64 * k : 64 * k + 64, :] = (centred * scale).reshape(64, 128)
        for s in range(SUB):
            hidden_t[:, s * 128 : (s + 1) * 128] = hidden[pl.ds(s, CH, stride=SUB), :].astype(jnp.bfloat16)
        for j in range(4):
            cols = slice(256 * j, 256 * (j + 1))
            update = jnp.dot(final_t[u], hidden_t[:, cols], preferred_element_type=jnp.float32)
            result = pair_t[:, cols] + gate[:, cols] * update
            pair_t[:, cols] = result.astype(jnp.bfloat16).astype(jnp.float32)

    for s in range(SUB):
        block = pair_t[:, s * 128 : (s + 1) * 128].T.astype(jnp.bfloat16)
        for q in range(4):
            out_ref[8 * q + s] = block[32 * q : 32 * q + 32]

    for u in range(2):

        @pl.loop(1, 16)
        def _(d):
            copy1(u, d).wait_send()
            copy3(u, d).wait_send()
            copy4(u, d).wait_send()

            @pl.loop(0, CHUNKS)
            def _(g):
                copy2(u, g, d).wait_send()


def shards(pair_act, residue_mask, *weights):
    bf16, f32 = jnp.bfloat16, jnp.float32
    dma = pltpu.SemaphoreType.DMA
    vmem = pl.BlockSpec(memory_space=pltpu.VMEM)
    return pl.pallas_call(
        kernel,
        out_shape=jax.ShapeDtypeStruct(pair_act.shape, pair_act.dtype),
        in_specs=[pl.BlockSpec(memory_space=pltpu.SMEM)] + [vmem] * 5,
        out_specs=vmem,
        scratch_shapes=[
            pltpu.VMEM((CH, 1024), f32),
            pltpu.VMEM((2, 5 * CH, CH), bf16),
            pltpu.VMEM((2, CH, CH), bf16),
            pltpu.VMEM((SUB, 128), f32),
            pltpu.VMEM((CH, 1024), bf16),
            pltpu.VMEM((5 * CH, 1024), f32),
            pltpu.VMEM((CH, 1024), f32),
            pltpu.VMEM((128, 128), f32),
            pltpu.VMEM((2, ROWS, 8, 16, 128), bf16),
            pltpu.VMEM((2, ROWS, 8, 16, 128), bf16),
            pltpu.VMEM((2, COLS, ROWS, 16, 128), bf16),
            pltpu.VMEM((256, 512), bf16),
            pltpu.VMEM((512, 256), bf16),
            pltpu.VMEM((512, 512), bf16),
            pltpu.VMEM((256, 512), f32),
            pltpu.VMEM((2, COLS, 64, 128), bf16),
            pltpu.VMEM((2, COLS, 64, 128), bf16),
            pltpu.VMEM((2, ROWS, 64, 128), bf16),
            pltpu.VMEM((2, ROWS, 64, 128), bf16),
            pltpu.VMEM((1024, 128), f32),
            pltpu.VMEM((CH, 1024), bf16),
            dma((2, ROWS)), dma((2, ROWS)),
            dma((2, CHUNKS, COLS)), dma((2, CHUNKS, COLS)),
            dma((2, COLS)), dma((2, COLS)),
            dma((2, ROWS)), dma((2, ROWS)),
        ],
        compiler_params=pltpu.CompilerParams(
            collective_id=0, has_side_effects=True, vmem_limit_bytes=48 * 1024 * 1024
        ),
    )(residue_mask, pair_act, *weights)


def solution(mesh):
    return jax.shard_map(
        shards,
        mesh=mesh,
        in_specs=(P("row", "col", None), P(), P(), P(), P(), P()),
        out_specs=P("row", "col", None),
        check_vma=False,
    )
```

time: 478 us -> 102 us (0.21)
  waiting for transfers between devices: 358 us -> 0 us
  Pallas kernels: 0 us -> 95.7 us
  local copies, waits for them, and re-layouts: 58.1 us -> 5.68 us
  starting transfers between devices: 22.9 us -> 0 us
  matrix products: 15.2 us -> 0 us
  between operations: 13.3 us -> 0.02 us
  other arithmetic: 7.14 us -> 0 us
    all_gather x4 -> x0, waiting for transfers between devices: 357 us -> none  [the longest x1 136 us: shards(): right_cols = lax.all_gather(right, 'row', axis=0, tiled=True)]
    pallas_call x0 -> x1, Pallas kernels: none -> 95.7 us  [shards(): pl.pallas_call(kernel, out_shape=jax.ShapeDtypeStruct(pair_act.shape, pai...]
    all_to_all x4 -> x0, local copies, waits for them, and re-layouts: 28 us -> none  [the longest x2 14.6 us: shards(): lax.all_to_all(left_whole, 'row', split_axis=1, concat_axis=0, tiled=True)]
    all_gather x3 -> x0, local copies, waits for them, and re-layouts: 23.4 us -> none  [the longest x1 8.57 us: shards(): right_cols = lax.all_gather(right, 'row', axis=0, tiled=True)]
    all_to_all x2 -> x0, starting transfers between devices: 22.8 us -> none  [the longest x1 15.9 us: shards(): lax.all_to_all(right_whole, 'col', split_axis=0, concat_axis=1, tiled=True)]
    dot_general x6 -> x0, matrix products: 15.2 us -> none  [the longest x1 4.69 us: shards(): jnp.einsum('ikh,jkh->ijh', left_rows, right_turned, preferred_element_typ...]
  transfers between devices with their start and end apart: 6 -> 0, of which waited for: 4 -> 0; matrix products, arithmetic and copies ran while one was open for 5% -> 0% of each run, Pallas kernels for 0% -> 0%
where the time goes in v1:
time: 102 us; the launch traced here: 101 us
  Pallas kernels  95.7 us (94%)
  local copies, waits for them, and re-layouts  5.68 us (6%)
    pallas_call x1, Pallas kernels, shards(): pl.pallas_call(kernel, out_shape=jax.ShapeDtypeStruct(pair_act.shape, pai...  95.7 us
    unnamed x13, local copies, waits for them, and re-layouts  5.68 us

profile of v1, /device:TPU:1, one launch (start us, length us, event | category | flops | bytes accessed | tf_op | source)
XLA Modules:
  0.0 101.4 jit_solution(4431755483724733530)
XLA Ops:
  0.0 0.0 copy-start
  0.0 0.9 copy-done
  1.0 0.0 copy-start.1
  1.0 0.9 copy-done.1
  1.9 0.0 copy-start.2
  1.9 0.9 copy-done.2
  2.8 0.0 copy-start.3
  2.8 0.8 copy-done.3
  3.5 0.0 copy-start.4
  3.5 0.8 copy-done.4
  4.3 0.0 copy-start.5
  4.3 0.7 copy-done.5
  5.0 95.7 %shard_map.64 = bf16[32,32,128]{2,1,0:T(8,128)(2,1)S(1)} custom-call(s32[512]{0:T(512)S(1)} %copy-done.5, bf16[32,32,128]{2,1,0:T(8,128)(2,1)S(1)} %copy-done, bf16[128,640]{1,0:T(8,128)(2,1)S(1)} %copy-done.1, bf16[128,128]{1,0:T(8,128)(2,1)S(1)} %copy-done.3, bf16[128,640]{1,0:T(8,128)(2,1)S(1)} %copy-done.2, bf16[128,128]{1,0:T(8,128)(2,1)S(1)} %copy-done.4), custom_call_target="tpu_custom_call" | custom-call | tf_op jit(solution)/shard_map/pallas_call | solution.py:319
  100.7 0.7 copy.8
Async XLA Ops:
  0.0 0.9 copy-start
  1.0 0.9 copy-start.1
  1.9 0.9 copy-start.2
  2.8 0.8 copy-start.3
  3.5 0.8 copy-start.4
  4.3 0.7 copy-start.5

commit v2 on v1

v2 whole, which is shorter than its diff:
```python
import jax
import jax.numpy as jnp
from jax import lax
from jax.experimental import pallas as pl
from jax.experimental.pallas import tpu as pltpu
from jax.sharding import PartitionSpec as P

ROWS = 16
COLS = 16
CH = 128
BLK = 32
SUB = 8
CHUNKS = 4
PER = ROWS // CHUNKS
STEPS = (4, 3, -3, 2, -2, 1, -1, 0)
ZERO = STEPS.index(0)
SELF = 2 * ZERO
MESH = pl.DeviceIdType.MESH


def block_transpose(parts):
    lane = lax.broadcasted_iota(jnp.int32, parts[0].shape, 1)
    low = lane < 64
    even = (lane // 32) % 2 == 0
    t0, t1, t2, t3 = parts
    u0 = jnp.where(low, t0, pltpu.roll(t2, 64, 1))
    u2 = jnp.where(low, pltpu.roll(t0, 64, 1), t2)
    u1 = jnp.where(low, t1, pltpu.roll(t3, 64, 1))
    u3 = jnp.where(low, pltpu.roll(t1, 64, 1), t3)
    return (
        jnp.where(even, u0, pltpu.roll(u1, 32, 1)),
        jnp.where(even, pltpu.roll(u0, 96, 1), u1),
        jnp.where(even, u2, pltpu.roll(u3, 32, 1)),
        jnp.where(even, pltpu.roll(u2, 96, 1), u3),
    )


def kernel(
    mask_hbm, pair_hbm, w_out, f_out, w_in, f_in, out_ref,
    mask_ref, pair_ref, w_ref, f_ref,
    pair_t, weights_t, final_t, half_mask, normed, mixed, gate, stage,
    send1, recv1, left_o, left_i, right, summed, send3, recv3,
    hidden, hidden_t,
    s0, s1, r1, sf, rf, s3, r3, sg, rg,
):
    loads = [
        pltpu.make_async_copy(src, dst, s0.at[i])
        for i, (src, dst) in enumerate(
            (
                (pair_hbm, pair_ref), (w_out, w_ref.at[0]), (mask_hbm, mask_ref),
                (w_in, w_ref.at[1]), (f_out, f_ref.at[0]), (f_in, f_ref.at[1]),
            )
        )
    ]
    for load in loads:
        load.start()

    row, col = lax.axis_index("row"), lax.axis_index("col")
    y_lo, z = row // 8, row % 8
    x, y_hi, core = col // 4, (col // 2) % 2, col % 2
    chip = col // 2
    z_to = [(z + b + 8) % 8 for b in STEPS]
    z_from = [(z + 8 - b) % 8 for b in STEPS]
    y_at = [y_lo, 1 - y_lo]
    x_at = [(x + e) % 4 for e in range(4)]
    y_hi_at = [y_hi, 1 - y_hi]
    row_to = [y_at[d % 2] * 8 + z_to[d // 2] for d in range(ROWS)]
    row_back = [core * 8 + z_to[b] for b in range(8)]
    row_from = [y_at[d % 2] * 8 + z_from[d // 2] for d in range(ROWS)]
    chip_to = [x_at[e // 2] * 2 + y_hi_at[e % 2] for e in range(8)]
    col_to = [chip_to[e] * 2 + core for e in range(8)]
    sibling = {"col": chip * 2 + 1 - core}
    entry = y_lo == core

    barrier = pltpu.get_barrier_semaphore()
    for d in range(ROWS):
        for e in range(8):
            if (d, e) != (SELF, 0):
                pl.semaphore_signal(
                    barrier, inc=1, device_id={"row": row_to[d], "col": col_to[e]}, device_id_type=MESH
                )
    pl.semaphore_signal(barrier, inc=1, device_id=sibling, device_id_type=MESH)

    def remote(src, dst, ssem, rsem, to):
        return pltpu.make_async_remote_copy(
            src_ref=src, dst_ref=dst, send_sem=ssem, recv_sem=rsem,
            device_id=to, device_id_type=MESH,
        )

    def copy1(u, d, e):
        src = send1.at[u, d, chip_to[e]]
        dst = recv1.at[u, core, d // PER, d % PER, chip]
        if (d, e) == (SELF, 0):
            return pltpu.make_async_copy(src, dst, r1.at[u, d // PER])
        return remote(
            src, dst, s1.at[u, d], r1.at[u, d // PER], {"row": row_to[d], "col": col_to[e]}
        )

    def wait1(u, g):
        block = recv1.at[u, core, g]
        remote(block, block, s1.at[u, 0], r1.at[u, g], sibling).wait_recv()

    def forward1(u, g):
        block = recv1.at[u, core, g]
        return remote(block, block, sf.at[u, g], rf.at[u, g], sibling)

    def copy3(u, b, e):
        return remote(
            send3.at[u, b, chip_to[e]], recv3.at[u, row, chip], s3.at[u, b, int((b, e) == (ZERO, 0))],
            r3.at[u, b // 2], {"row": row_back[b], "col": col_to[e]},
        )

    def wait3(u, k):
        block = recv3.at[u, pl.ds(4 * k, 4)]
        remote(block, block, s3.at[u, 0, 0], r3.at[u, k], sibling).wait_recv()

    def forward3(u, d):
        block = recv3.at[u, row_from[d]]
        return remote(block, block, sg.at[u, d], rg.at[u, d], sibling)

    def turn_weights(u):
        weights_t[u] = w_ref[u].astype(jnp.float32).T.astype(jnp.bfloat16)

    loads[0].wait()
    for s in range(SUB):
        block = jnp.concatenate([pair_ref[8 * q + s] for q in range(4)], axis=0)
        pair_t[:, s * 128 : (s + 1) * 128] = block.astype(jnp.float32).T
    loads[1].wait()
    turn_weights(0)

    loads[2].wait()
    lane = lax.broadcasted_iota(jnp.int32, (SUB, 128), 1)
    sub = lax.broadcasted_iota(jnp.int32, (SUB, 128), 0)
    by_row = jnp.zeros((SUB, 128), jnp.float32)
    by_col = jnp.zeros((SUB, 128), jnp.float32)
    for k in range(BLK):
        by_col = jnp.where(lane % 32 == k, mask_ref[col * BLK + k].astype(jnp.float32), by_col)
        by_row = jnp.where(
            (lane // 32) * 8 + sub == k, mask_ref[row * BLK + k].astype(jnp.float32), by_row
        )
    half_mask[...] = 0.5 * by_row * by_col

    def project(u):
        for j in range(4):
            cols = slice(256 * j, 256 * (j + 1))
            values = pair_t[:, cols]
            middle = jnp.mean(values, axis=0, keepdims=True)
            centred = values - middle
            spread = jnp.mean(centred * centred, axis=0, keepdims=True)
            normed[:, cols] = (centred * lax.rsqrt(spread + 1e-05)).astype(jnp.bfloat16)
            mixed[:, cols] = jnp.dot(
                weights_t[u], normed[:, cols], preferred_element_type=jnp.float32
            )

    def sides(u, d):
        at = row_to[d] * 8
        held = stage.at[d % 2]

        def part(k):
            return mixed[pl.ds(pl.multiple_of(at + k * CH, 8), 8), :]

        for side in range(2):
            value, gates = part(2 * side), part(2 * side + 1)
            for s in range(SUB):
                cols = slice(s * 128, (s + 1) * 128)
                held[pl.ds(side * 8 + s, 8, stride=16), :] = (
                    (jnp.tanh(0.5 * gates[:, cols]) + 1.0) * value[:, cols] * half_mask[s : s + 1, :]
                )
        return held[...].astype(jnp.bfloat16).reshape(8, 16, 128)

    def tile_at(u, g, cc, t, i):
        return recv1[u, t % 2, g, i, 2 * cc + t // 2].astype(jnp.float32)

    def assemble_right(u, g):
        for cc in range(4):
            turned = block_transpose(
                [jnp.concatenate([tile_at(u, g, cc, t, i)[8:] for i in range(PER)], axis=0) for t in range(4)]
            )
            for i in range(PER):
                rows = jnp.concatenate([v[8 * i : 8 * i + 8] for v in turned], axis=0)
                at = pl.multiple_of(row_from[g * PER + i] * BLK, BLK)
                right[pl.ds(at, BLK), cc * 128 : (cc + 1) * 128] = rows.astype(jnp.bfloat16)

    def assemble_left_o(u, g):
        a = (core + y_lo) % 2
        for cc in range(4):
            turned = block_transpose(
                [
                    jnp.concatenate([tile_at(u, g, cc, t, 2 * i + a)[:8] for i in range(PER // 2)], axis=0)
                    for t in range(4)
                ]
            )
            for i in range(PER // 2):
                rows = jnp.concatenate([v[8 * i : 8 * i + 8] for v in turned], axis=0)
                at = pl.multiple_of(z_from[g * PER // 2 + i] * BLK, BLK)
                left_o[pl.ds(at, BLK), cc * 128 : (cc + 1) * 128] = rows.astype(jnp.bfloat16)

    def assemble_left_i(u, g):
        for cc in range(2):
            turned = block_transpose(
                [
                    jnp.concatenate([tile_at(u, g, 2 * core + cc, t, i)[:8] for i in range(PER)], axis=0)
                    for t in range(4)
                ]
            )
            for i in range(PER):
                rows = jnp.concatenate([v[8 * i : 8 * i + 8] for v in turned], axis=0)
                at = pl.multiple_of(row_from[g * PER + i] * BLK, BLK)
                left_i[pl.ds(at, BLK), cc * 128 : (cc + 1) * 128] = rows.astype(jnp.bfloat16)

    def assemble(u, g):
        forward1(u, g).wait_recv()
        assemble_right(u, g)
        if u == 0:
            assemble_left_o(u, g)
        else:
            assemble_left_i(u, g)

    for u in range(2):
        project(u)
        if u == 0:
            pl.semaphore_wait(barrier, 128)

        for d in range(ROWS):
            send1[u, d] = sides(u, d)
            for e in range(8):
                copy1(u, d, e).start()

        gate[...] = 0.5 * jnp.tanh(0.5 * mixed[4 * CH :, :]) + 0.5
        if u == 0:
            for load in loads[3:]:
                load.wait()
            turn_weights(1)
            for k in range(2):
                final_t[k] = f_ref[k].astype(jnp.float32).T.astype(jnp.bfloat16)

        for g in range(CHUNKS):
            wait1(u, g)
            forward1(u, g).start()
            if g >= 1:
                assemble(u, g - 1)
        assemble(u, CHUNKS - 1)

        if u == 0:
            summed[...] = lax.dot_general(
                left_o[...], right[...], (((1,), (1,)), ((), ())), preferred_element_type=jnp.float32
            )
        else:
            summed[...] = lax.dot_general(
                left_i[...], right[...], (((0,), (0,)), ((), ())), preferred_element_type=jnp.float32
            )

        for b in range(8):
            for cc in range(4):
                turned = block_transpose(
                    [
                        summed[
                            pl.ds(pl.multiple_of(z_to[b] * BLK + 8 * q, 8), 8),
                            cc * 128 : (cc + 1) * 128,
                        ]
                        for q in range(4)
                    ]
                )
                for k in range(2):
                    tile = jnp.concatenate(turned[2 * k : 2 * k + 2], axis=0)
                    send3[u, b, 2 * cc + k] = tile.astype(jnp.bfloat16)
            for e in range(8):
                if (b, e) != (ZERO, 0):
                    copy3(u, b, e).start()
                else:

                    @pl.when(entry)
                    def _():
                        own = pltpu.make_async_copy(
                            send3.at[u, b, chip], recv3.at[u, row, chip], r3.at[u, b // 2]
                        )
                        own.start()

                    @pl.when(jnp.logical_not(entry))
                    def _():
                        copy3(u, b, e).start()

        @pl.when(entry)
        def _():
            for k in range(4):
                wait3(u, k)
                for d in range(4 * k, 4 * k + 4):
                    forward3(u, d).start()

        @pl.when(jnp.logical_not(entry))
        def _():
            for d in range(ROWS):
                forward3(u, d).wait_recv()

        def sums(k):
            both = recv3[u, k].astype(jnp.float32)
            return jnp.where(core == 0, both[:, :8], both[:, 8:])

        total = jnp.zeros((SUB, 128), jnp.float32)
        for k in range(ROWS):
            total += jnp.sum(sums(k), axis=0)
        middle = total * (1.0 / CH)
        total = jnp.zeros((SUB, 128), jnp.float32)
        for k in range(ROWS):
            centred = sums(k) - middle
            total += jnp.sum(centred * centred, axis=0)
        scale = lax.rsqrt(total * (1.0 / CH) + 1e-05)
        for k in range(ROWS):
            centred = sums(k) - middle
            hidden[64 * k : 64 * k + 64, :] = (centred * scale).reshape(64, 128)
        for s in range(SUB):
            hidden_t[:, s * 128 : (s + 1) * 128] = hidden[pl.ds(s, CH, stride=SUB), :].astype(jnp.bfloat16)
        for j in range(4):
            cols = slice(256 * j, 256 * (j + 1))
            update = jnp.dot(final_t[u], hidden_t[:, cols], preferred_element_type=jnp.float32)
            result = pair_t[:, cols] + gate[:, cols] * update
            pair_t[:, cols] = result.astype(jnp.bfloat16).astype(jnp.float32)

    for s in range(SUB):
        block = pair_t[:, s * 128 : (s + 1) * 128].T.astype(jnp.bfloat16)
        for q in range(4):
            out_ref[8 * q + s] = block[32 * q : 32 * q + 32]

    for u in range(2):
        for d in range(ROWS):
            count = 7 if d == SELF else 8
            remote(
                send1.at[u, d, pl.ds(0, count)], send1.at[u, d, pl.ds(0, count)],
                s1.at[u, d], r1.at[u, 0], sibling,
            ).wait_send()
        for g in range(CHUNKS):
            forward1(u, g).wait_send()
        for b in range(8):
            count = 7 if b == ZERO else 8
            remote(
                send3.at[u, b, pl.ds(0, count)], send3.at[u, b, pl.ds(0, count)],
                s3.at[u, b, 0], r3.at[u, 0], sibling,
            ).wait_send()

        @pl.when(entry)
        def _():
            for d in range(ROWS):
                forward3(u, d).wait_send()

        @pl.when(jnp.logical_not(entry))
        def _():
            copy3(u, ZERO, 0).wait_send()


def shards(pair_act, residue_mask, *weights):
    bf16, f32 = jnp.bfloat16, jnp.float32
    dma = pltpu.SemaphoreType.DMA
    vmem = pl.BlockSpec(memory_space=pltpu.VMEM)
    return pl.pallas_call(
        kernel,
        out_shape=jax.ShapeDtypeStruct(pair_act.shape, pair_act.dtype),
        in_specs=[pl.BlockSpec(memory_space=pl.ANY)] * 6,
        out_specs=vmem,
        scratch_shapes=[
            pltpu.SMEM(residue_mask.shape, jnp.int32),
            pltpu.VMEM(pair_act.shape, bf16),
            pltpu.VMEM((2, CH, 5 * CH), bf16),
            pltpu.VMEM((2, CH, CH), bf16),
            pltpu.VMEM((CH, 1024), f32),
            pltpu.VMEM((2, 5 * CH, CH), bf16),
            pltpu.VMEM((2, CH, CH), bf16),
            pltpu.VMEM((SUB, 128), f32),
            pltpu.VMEM((CH, 1024), bf16),
            pltpu.VMEM((5 * CH, 1024), f32),
            pltpu.VMEM((CH, 1024), f32),
            pltpu.VMEM((2, 128, 128), f32),
            pltpu.VMEM((2, ROWS, 8, 16, 128), bf16),
            pltpu.VMEM((2, 2, CHUNKS, PER, 8, 16, 128), bf16),
            pltpu.VMEM((256, 512), bf16),
            pltpu.VMEM((512, 256), bf16),
            pltpu.VMEM((512, 512), bf16),
            pltpu.VMEM((256, 512), f32),
            pltpu.VMEM((2, 8, 8, 16, 128), bf16),
            pltpu.VMEM((2, ROWS, 8, 16, 128), bf16),
            pltpu.VMEM((1024, 128), f32),
            pltpu.VMEM((CH, 1024), bf16),
            dma((6,)),
            dma((2, ROWS)), dma((2, CHUNKS)),
            dma((2, CHUNKS)), dma((2, CHUNKS)),
            dma((2, 8, 2)), dma((2, 4)),
            dma((2, ROWS)), dma((2, ROWS)),
        ],
        compiler_params=pltpu.CompilerParams(
            collective_id=0, has_side_effects=True, vmem_limit_bytes=60 * 1024 * 1024
        ),
    )(residue_mask, pair_act, *weights)


def solution(mesh):
    return jax.shard_map(
        shards,
        mesh=mesh,
        in_specs=(P("row", "col", None), P(), P(), P(), P(), P()),
        out_specs=P("row", "col", None),
        check_vma=False,
    )
```

time: 102 us -> 77.5 us (0.76)
  Pallas kernels: 95.7 us -> 75.7 us
  local copies, waits for them, and re-layouts: 5.68 us -> 1.67 us
    pallas_call x1, Pallas kernels: 95.7 us -> 75.7 us  [shards(): pl.pallas_call(kernel, out_shape=jax.ShapeDtypeStruct(pair_act.shape, pai...]
    unnamed x13 -> x1, local copies, waits for them, and re-layouts: 5.68 us -> 1.67 us
where the time goes in v2:
time: 77.5 us; the launch traced here: 77.4 us
  Pallas kernels  75.7 us (98%)
  local copies, waits for them, and re-layouts  1.67 us (2%)
    pallas_call x1, Pallas kernels, shards(): pl.pallas_call(kernel, out_shape=jax.ShapeDtypeStruct(pair_act.shape, pai...  75.7 us
    unnamed x1, local copies, waits for them, and re-layouts  1.67 us

profile of v2, /device:TPU:1, one launch (start us, length us, event | category | flops | bytes accessed | tf_op | source)
XLA Modules:
  0.0 77.4 jit_solution(14109414849671497031)
XLA Ops:
  0.0 75.7 %shard_map.64 = bf16[32,32,128]{2,1,0:T(8,128)(2,1)} custom-call(s32[512]{0:T(512)} %mask_hbm.1, bf16[32,32,128]{2,1,0:T(8,128)(2,1)} %pair_hbm.1, bf16[128,640]{1,0:T(8,128)(2,1)} %w_out.1, bf16[128,128]{1,0:T(8,128)(2,1)} %f_out.1, bf16[128,640]{1,0:T(8,128)(2,1)} %w_in.1, bf16[128,128]{1,0:T(8,128)(2,1)} %f_in.1), custom_call_target="tpu_custom_call" | custom-call | tf_op jit(solution)/shard_map/pallas_call | solution.py:354
  75.7 1.7 %copy.8 = bf16[32,32,128]{2,1,0:T(8,128)(2,1)} copy(bf16[32,32,128]{2,1,0:T(8,128)(2,1)} %shard_map.64) | data formatting | bytes 524288

commit v3 on v2

--- a/solution.py
+++ b/solution.py
@@ -13,8 +13,9 @@
 CHUNKS = 4
 PER = ROWS // CHUNKS
 STEPS = (4, 3, -3, 2, -2, 1, -1, 0)
-ZERO = STEPS.index(0)
-SELF = 2 * ZERO
+SELF = 2 * STEPS.index(0)
+EVEN, ODD = (4, 2, -2, 0), (3, -3, 1, -1)
+LAST = 2 * EVEN.index(0)
 MESH = pl.DeviceIdType.MESH
 
 
@@ -39,9 +40,9 @@
     mask_hbm, pair_hbm, w_out, f_out, w_in, f_in, out_ref,
     mask_ref, pair_ref, w_ref, f_ref,
     pair_t, weights_t, final_t, half_mask, normed, mixed, gate, stage,
-    send1, recv1, left_o, left_i, right, summed, send3, recv3,
+    send1, recv1, left, right_o, right_i, summed, send3, recv3,
     hidden, hidden_t,
-    s0, s1, r1, sf, rf, s3, r3, sg, rg,
+    s0, s1, r1, sf, rf, s3, r3, sx,
 ):
     loads = [
         pltpu.make_async_copy(src, dst, s0.at[i])
@@ -62,15 +63,19 @@
     z_to = [(z + b + 8) % 8 for b in STEPS]
     z_from = [(z + 8 - b) % 8 for b in STEPS]
     y_at = [y_lo, 1 - y_lo]
+    core_at = [core, 1 - core]
     x_at = [(x + e) % 4 for e in range(4)]
     y_hi_at = [y_hi, 1 - y_hi]
     row_to = [y_at[d % 2] * 8 + z_to[d // 2] for d in range(ROWS)]
-    row_back = [core * 8 + z_to[b] for b in range(8)]
+    odd = [(z + core) % 2, (z + core + 1) % 2]
+    z_part = [
+        [(z + 8 + EVEN[j] + odd[part] * (ODD[j] - EVEN[j])) % 8 for j in range(4)] for part in range(2)
+    ]
+    row_part = [[y_at[k % 2] * 8 + z_part[part][k // 2] for k in range(8)] for part in range(2)]
     row_from = [y_at[d % 2] * 8 + z_from[d // 2] for d in range(ROWS)]
     chip_to = [x_at[e // 2] * 2 + y_hi_at[e % 2] for e in range(8)]
     col_to = [chip_to[e] * 2 + core for e in range(8)]
     sibling = {"col": chip * 2 + 1 - core}
-    entry = y_lo == core
 
     barrier = pltpu.get_barrier_semaphore()
     for d in range(ROWS):
@@ -98,25 +103,33 @@
 
     def wait1(u, g):
         block = recv1.at[u, core, g]
-        remote(block, block, s1.at[u, 0], r1.at[u, g], sibling).wait_recv()
+        remote(block, block, sx, r1.at[u, g], sibling).wait_recv()
 
     def forward1(u, g):
-        block = recv1.at[u, core, g]
+        block = recv1.at[u, core, g] if u == 0 else recv1.at[u, core, g, :, :, 0]
         return remote(block, block, sf.at[u, g], rf.at[u, g], sibling)
 
-    def copy3(u, b, e):
-        return remote(
-            send3.at[u, b, chip_to[e]], recv3.at[u, row, chip], s3.at[u, b, int((b, e) == (ZERO, 0))],
-            r3.at[u, b // 2], {"row": row_back[b], "col": col_to[e]},
-        )
-
-    def wait3(u, k):
-        block = recv3.at[u, pl.ds(4 * k, 4)]
-        remote(block, block, s3.at[u, 0, 0], r3.at[u, k], sibling).wait_recv()
-
-    def forward3(u, d):
-        block = recv3.at[u, row_from[d]]
-        return remote(block, block, sg.at[u, d], rg.at[u, d], sibling)
+    def send_sums(u, slot, to_row, e, own):
+        src, dst = send3.at[u, slot, chip_to[e]], recv3.at[u, row, chip]
+        to = {"row": to_row, "col": col_to[e]}
+
+        def here():
+            pltpu.make_async_copy(src, dst, r3.at[u]).start()
+
+        if own is None:
+            remote(src, dst, s3.at[u, slot], r3.at[u], to).start()
+        elif own is True:
+            here()
+        else:
+            pl.when(own)(here)
+
+            @pl.when(jnp.logical_not(own))
+            def _():
+                remote(src, dst, sx, r3.at[u], to).start()
+
+    def wait_sums(u):
+        block = recv3.at[u]
+        remote(block, block, sx, r3.at[u], sibling).wait_recv()
 
     def turn_weights(u):
         weights_t[u] = w_ref[u].astype(jnp.float32).T.astype(jnp.bfloat16)
@@ -166,55 +179,53 @@
                 held[pl.ds(side * 8 + s, 8, stride=16), :] = (
                     (jnp.tanh(0.5 * gates[:, cols]) + 1.0) * value[:, cols] * half_mask[s : s + 1, :]
                 )
-        return held[...].astype(jnp.bfloat16).reshape(8, 16, 128)
-
-    def tile_at(u, g, cc, t, i):
-        return recv1[u, t % 2, g, i, 2 * cc + t // 2].astype(jnp.float32)
-
-    def assemble_right(u, g):
-        for cc in range(4):
-            turned = block_transpose(
-                [jnp.concatenate([tile_at(u, g, cc, t, i)[8:] for i in range(PER)], axis=0) for t in range(4)]
-            )
-            for i in range(PER):
-                rows = jnp.concatenate([v[8 * i : 8 * i + 8] for v in turned], axis=0)
-                at = pl.multiple_of(row_from[g * PER + i] * BLK, BLK)
-                right[pl.ds(at, BLK), cc * 128 : (cc + 1) * 128] = rows.astype(jnp.bfloat16)
-
-    def assemble_left_o(u, g):
-        a = (core + y_lo) % 2
-        for cc in range(4):
+        return held[...].astype(jnp.bfloat16).reshape(8, 2, SUB, 128)
+
+    def turned_tiles(u, k, g, slots, v, side):
+        turned = block_transpose(
+            [
+                jnp.concatenate(
+                    [recv1[u, k, g, i, 4 * v + t, side].astype(jnp.float32) for i in slots], axis=0
+                )
+                for t in range(4)
+            ]
+        )
+        return [
+            jnp.concatenate([w[8 * i : 8 * i + 8] for w in turned], axis=0).astype(jnp.bfloat16)
+            for i in range(len(slots))
+        ]
+
+    def band(r):
+        return pl.ds(pl.multiple_of(r * BLK, BLK), BLK)
+
+    def assemble(u, g, part):
+        k = core_at[part]
+        for v in range(2):
+            lanes = slice(256 * part + 128 * v, 256 * part + 128 * v + 128)
+            for i, rows in enumerate(turned_tiles(u, k, g, range(PER), v, 0)):
+                left[band(row_from[g * PER + i]), lanes] = rows
+            if u == 0:
+                step = (z + core + g) % 2
+                z_src = z_from[2 * g] + step * (z_from[2 * g + 1] - z_from[2 * g])
+                slots = [2 * step + a for a in range(2)]
+                for a, rows in enumerate(turned_tiles(u, k, g, slots, v, 1)):
+                    right_o[band(y_at[a] * 4 + z_src // 2), lanes] = rows
+            elif part == 0:
+                for i, rows in enumerate(turned_tiles(u, k, g, range(PER), v, 1)):
+                    right_i[band(row_from[g * PER + i]), lanes] = rows
+
+    def back(u, slot, to_row, at, own):
+        for v in range(2):
             turned = block_transpose(
                 [
-                    jnp.concatenate([tile_at(u, g, cc, t, 2 * i + a)[:8] for i in range(PER // 2)], axis=0)
-                    for t in range(4)
+                    summed[pl.ds(pl.multiple_of(at + 8 * q, 8), 8), 128 * v : 128 * v + 128]
+                    for q in range(4)
                 ]
             )
-            for i in range(PER // 2):
-                rows = jnp.concatenate([v[8 * i : 8 * i + 8] for v in turned], axis=0)
-                at = pl.multiple_of(z_from[g * PER // 2 + i] * BLK, BLK)
-                left_o[pl.ds(at, BLK), cc * 128 : (cc + 1) * 128] = rows.astype(jnp.bfloat16)
-
-    def assemble_left_i(u, g):
-        for cc in range(2):
-            turned = block_transpose(
-                [
-                    jnp.concatenate([tile_at(u, g, 2 * core + cc, t, i)[:8] for i in range(PER)], axis=0)
-                    for t in range(4)
-                ]
-            )
-            for i in range(PER):
-                rows = jnp.concatenate([v[8 * i : 8 * i + 8] for v in turned], axis=0)
-                at = pl.multiple_of(row_from[g * PER + i] * BLK, BLK)
-                left_i[pl.ds(at, BLK), cc * 128 : (cc + 1) * 128] = rows.astype(jnp.bfloat16)
-
-    def assemble(u, g):
-        forward1(u, g).wait_recv()
-        assemble_right(u, g)
-        if u == 0:
-            assemble_left_o(u, g)
-        else:
-            assemble_left_i(u, g)
+            for t, tile in enumerate(turned):
+                send3[u, slot, 4 * v + t] = tile.astype(jnp.bfloat16)
+        for e in range(8):
+            send_sums(u, slot, to_row, e, own if e == 0 else None)
 
     for u in range(2):
         project(u)
@@ -237,64 +248,42 @@
         for g in range(CHUNKS):
             wait1(u, g)
             forward1(u, g).start()
-            if g >= 1:
-                assemble(u, g - 1)
-        assemble(u, CHUNKS - 1)
+            assemble(u, g, 0)
 
         if u == 0:
-            summed[...] = lax.dot_general(
-                left_o[...], right[...], (((1,), (1,)), ((), ())), preferred_element_type=jnp.float32
-            )
+            for part in range(2):
+                if part == 1:
+                    for g in range(CHUNKS):
+                        forward1(u, g).wait_recv()
+                        assemble(u, g, 1)
+                lanes = slice(256 * part, 256 * part + 256)
+                term = lax.dot_general(
+                    left[:, lanes], right_o[:, lanes], (((1,), (1,)), ((), ())),
+                    preferred_element_type=jnp.float32,
+                )
+                summed[...] = term if part == 0 else summed[...] + term
+            for d in range(ROWS):
+                back(u, d, row_to[d], row_to[d] * BLK, True if d == SELF else None)
         else:
-            summed[...] = lax.dot_general(
-                left_i[...], right[...], (((0,), (0,)), ((), ())), preferred_element_type=jnp.float32
-            )
-
-        for b in range(8):
-            for cc in range(4):
-                turned = block_transpose(
-                    [
-                        summed[
-                            pl.ds(pl.multiple_of(z_to[b] * BLK + 8 * q, 8), 8),
-                            cc * 128 : (cc + 1) * 128,
-                        ]
-                        for q in range(4)
-                    ]
-                )
-                for k in range(2):
-                    tile = jnp.concatenate(turned[2 * k : 2 * k + 2], axis=0)
-                    send3[u, b, 2 * cc + k] = tile.astype(jnp.bfloat16)
-            for e in range(8):
-                if (b, e) != (ZERO, 0):
-                    copy3(u, b, e).start()
-                else:
-
-                    @pl.when(entry)
-                    def _():
-                        own = pltpu.make_async_copy(
-                            send3.at[u, b, chip], recv3.at[u, row, chip], r3.at[u, b // 2]
-                        )
-                        own.start()
-
-                    @pl.when(jnp.logical_not(entry))
-                    def _():
-                        copy3(u, b, e).start()
-
-        @pl.when(entry)
-        def _():
-            for k in range(4):
-                wait3(u, k)
-                for d in range(4 * k, 4 * k + 4):
-                    forward3(u, d).start()
-
-        @pl.when(jnp.logical_not(entry))
-        def _():
-            for d in range(ROWS):
-                forward3(u, d).wait_recv()
+            for part in range(2):
+                if part == 1:
+                    for g in range(CHUNKS):
+                        forward1(u, g).wait_recv()
+                        assemble(u, g, 1)
+                lanes = slice(256 * part, 256 * part + 256)
+                summed[lanes, :] = lax.dot_general(
+                    left[:, lanes], right_i[...], (((0,), (0,)), ((), ())),
+                    preferred_element_type=jnp.float32,
+                )
+                for k in range(8):
+                    at = 256 * part + (y_at[k % 2] * 4 + z_part[part][k // 2] // 2) * BLK
+                    own = odd[part] == 0 if k == LAST else None
+                    back(u, 8 * part + k, row_part[part][k], at, own)
+
+        wait_sums(u)
 
         def sums(k):
-            both = recv3[u, k].astype(jnp.float32)
-            return jnp.where(core == 0, both[:, :8], both[:, 8:])
+            return recv3[u, k].astype(jnp.float32)
 
         total = jnp.zeros((SUB, 128), jnp.float32)
         for k in range(ROWS):
@@ -330,21 +319,11 @@
             ).wait_send()
         for g in range(CHUNKS):
             forward1(u, g).wait_send()
-        for b in range(8):
-            count = 7 if b == ZERO else 8
-            remote(
-                send3.at[u, b, pl.ds(0, count)], send3.at[u, b, pl.ds(0, count)],
-                s3.at[u, b, 0], r3.at[u, 0], sibling,
-            ).wait_send()
-
-        @pl.when(entry)
-        def _():
-            for d in range(ROWS):
-                forward3(u, d).wait_send()
-
-        @pl.when(jnp.logical_not(entry))
-        def _():
-            copy3(u, ZERO, 0).wait_send()
+        for slot in range(ROWS):
+            count = 7 if slot in ((SELF,), (LAST, 8 + LAST))[u] else 8
+            block = send3.at[u, slot, pl.ds(0, count)]
+            remote(block, block, s3.at[u, slot], r3.at[u], sibling).wait_send()
+    remote(send3.at[1, 0, 0], send3.at[1, 0, 0], sx, r3.at[1], sibling).wait_send()
 
 
 def shards(pair_act, residue_mask, *weights):
@@ -369,21 +348,20 @@
             pltpu.VMEM((5 * CH, 1024), f32),
             pltpu.VMEM((CH, 1024), f32),
             pltpu.VMEM((2, 128, 128), f32),
-            pltpu.VMEM((2, ROWS, 8, 16, 128), bf16),
-            pltpu.VMEM((2, 2, CHUNKS, PER, 8, 16, 128), bf16),
+            pltpu.VMEM((2, ROWS, 8, 2, SUB, 128), bf16),
+            pltpu.VMEM((2, 2, CHUNKS, PER, 8, 2, SUB, 128), bf16),
+            pltpu.VMEM((512, 512), bf16),
             pltpu.VMEM((256, 512), bf16),
             pltpu.VMEM((512, 256), bf16),
-            pltpu.VMEM((512, 512), bf16),
-            pltpu.VMEM((256, 512), f32),
-            pltpu.VMEM((2, 8, 8, 16, 128), bf16),
-            pltpu.VMEM((2, ROWS, 8, 16, 128), bf16),
+            pltpu.VMEM((512, 256), f32),
+            pltpu.VMEM((2, ROWS, 8, SUB, 128), bf16),
+            pltpu.VMEM((2, ROWS, 8, SUB, 128), bf16),
             pltpu.VMEM((1024, 128), f32),
             pltpu.VMEM((CH, 1024), bf16),
             dma((6,)),
             dma((2, ROWS)), dma((2, CHUNKS)),
             dma((2, CHUNKS)), dma((2, CHUNKS)),
-            dma((2, 8, 2)), dma((2, 4)),
-            dma((2, ROWS)), dma((2, ROWS)),
+            dma((2, ROWS)), dma((2,)), dma,
         ],
         compiler_params=pltpu.CompilerParams(
             collective_id=0, has_side_effects=True, vmem_limit_bytes=60 * 1024 * 1024

time: 77.5 us -> 72.5 us (0.935)
  Pallas kernels: 75.7 us -> 70.7 us
    pallas_call x1, Pallas kernels: 75.7 us -> 70.7 us  [shards(): pl.pallas_call(kernel, out_shape=jax.ShapeDtypeStruct(pair_act.shape, pai...]
where the time goes in v3:
time: 72.5 us; the launch traced here: 72.4 us
  Pallas kernels  70.7 us (98%)
  local copies, waits for them, and re-layouts  1.67 us (2%)
    pallas_call x1, Pallas kernels, shards(): pl.pallas_call(kernel, out_shape=jax.ShapeDtypeStruct(pair_act.shape, pai...  70.7 us
    unnamed x1, local copies, waits for them, and re-layouts  1.67 us

profile of v3, /device:TPU:1, one launch (start us, length us, event | category | flops | bytes accessed | tf_op | source)
XLA Modules:
  0.0 72.4 jit_solution(4391625009232912258)
XLA Ops:
  0.0 70.7 %shard_map.64 = bf16[32,32,128]{2,1,0:T(8,128)(2,1)} custom-call(s32[512]{0:T(512)} %mask_hbm.1, bf16[32,32,128]{2,1,0:T(8,128)(2,1)} %pair_hbm.1, bf16[128,640]{1,0:T(8,128)(2,1)} %w_out.1, bf16[128,128]{1,0:T(8,128)(2,1)} %f_out.1, bf16[128,640]{1,0:T(8,128)(2,1)} %w_in.1, bf16[128,128]{1,0:T(8,128)(2,1)} %f_in.1), custom_call_target="tpu_custom_call" | custom-call | tf_op jit(solution)/shard_map/pallas_call | solution.py:333
  70.8 1.7 %copy.8 = bf16[32,32,128]{2,1,0:T(8,128)(2,1)} copy(bf16[32,32,128]{2,1,0:T(8,128)(2,1)} %shard_map.64) | data formatting | bytes 524288

commit v4 on v3

--- a/solution.py
+++ b/solution.py
@@ -17,6 +17,14 @@
 EVEN, ODD = (4, 2, -2, 0), (3, -3, 1, -1)
 LAST = 2 * EVEN.index(0)
 MESH = pl.DeviceIdType.MESH
+
+
+def far_first(slots, steps=STEPS):
+    def hops(to):
+        d, e = to
+        return abs(steps[d // 2]) + (0, 1, 2, 1)[e // 2] + ((0, 2), (1, 1))[d % 2][e % 2]
+
+    return sorted(((d, e) for d in slots for e in range(8)), key=hops, reverse=True)
 
 
 def block_transpose(parts):
@@ -185,13 +193,13 @@
         turned = block_transpose(
             [
                 jnp.concatenate(
-                    [recv1[u, k, g, i, 4 * v + t, side].astype(jnp.float32) for i in slots], axis=0
+                    [recv1[u, k, g, i, 4 * v + t, side] for i in slots], axis=0
                 )
                 for t in range(4)
             ]
         )
         return [
-            jnp.concatenate([w[8 * i : 8 * i + 8] for w in turned], axis=0).astype(jnp.bfloat16)
+            jnp.concatenate([w[8 * i : 8 * i + 8] for w in turned], axis=0)
             for i in range(len(slots))
         ]
 
@@ -214,27 +222,34 @@
                 for i, rows in enumerate(turned_tiles(u, k, g, range(PER), v, 1)):
                     right_i[band(row_from[g * PER + i]), lanes] = rows
 
-    def back(u, slot, to_row, at, own):
+    def turn_sums(u, slots, at):
         for v in range(2):
             turned = block_transpose(
                 [
-                    summed[pl.ds(pl.multiple_of(at + 8 * q, 8), 8), 128 * v : 128 * v + 128]
+                    jnp.concatenate(
+                        [
+                            summed[pl.ds(pl.multiple_of(a + 8 * q, 8), 8), 128 * v : 128 * v + 128]
+                            for a in at
+                        ],
+                        axis=0,
+                    )
                     for q in range(4)
                 ]
             )
-            for t, tile in enumerate(turned):
-                send3[u, slot, 4 * v + t] = tile.astype(jnp.bfloat16)
-        for e in range(8):
-            send_sums(u, slot, to_row, e, own if e == 0 else None)
+            for t, tiles in enumerate(turned):
+                for i, slot in enumerate(slots):
+                    send3[u, slot, 4 * v + t] = tiles[8 * i : 8 * i + 8].astype(jnp.bfloat16)
 
     for u in range(2):
         project(u)
         if u == 0:
             pl.semaphore_wait(barrier, 128)
 
-        for d in range(ROWS):
-            send1[u, d] = sides(u, d)
-            for e in range(8):
+        for g in range(CHUNKS):
+            slots = range(g * PER, (g + 1) * PER)
+            for d in slots:
+                send1[u, d] = sides(u, d)
+            for d, e in far_first(slots):
                 copy1(u, d, e).start()
 
         gate[...] = 0.5 * jnp.tanh(0.5 * mixed[4 * CH :, :]) + 0.5
@@ -262,8 +277,11 @@
                     preferred_element_type=jnp.float32,
                 )
                 summed[...] = term if part == 0 else summed[...] + term
-            for d in range(ROWS):
-                back(u, d, row_to[d], row_to[d] * BLK, True if d == SELF else None)
+            for g in range(4):
+                slots = range(4 * g, 4 * g + 4)
+                turn_sums(u, slots, [row_to[d] * BLK for d in slots])
+            for d, e in far_first(range(ROWS)):
+                send_sums(u, d, row_to[d], e, True if (d, e) == (SELF, 0) else None)
         else:
             for part in range(2):
                 if part == 1:
@@ -275,10 +293,15 @@
                     left[:, lanes], right_i[...], (((0,), (0,)), ((), ())),
                     preferred_element_type=jnp.float32,
                 )
-                for k in range(8):
-                    at = 256 * part + (y_at[k % 2] * 4 + z_part[part][k // 2] // 2) * BLK
-                    own = odd[part] == 0 if k == LAST else None
-                    back(u, 8 * part + k, row_part[part][k], at, own)
+                for g in range(2):
+                    slots = range(4 * g, 4 * g + 4)
+                    turn_sums(
+                        u, [8 * part + k for k in slots],
+                        [256 * part + (y_at[k % 2] * 4 + z_part[part][k // 2] // 2) * BLK for k in slots],
+                    )
+                for k, e in far_first(range(8), (3.5, 2.5, 1.5, 0.5)):
+                    own = odd[part] == 0 if (k, e) == (LAST, 0) else None
+                    send_sums(u, 8 * part + k, row_part[part][k], e, own)
 
         wait_sums(u)
 

time: 72.5 us -> 70.7 us (0.975)
  Pallas kernels: 70.7 us -> 68.9 us
    pallas_call x1, Pallas kernels: 70.7 us -> 68.9 us  [shards(): pl.pallas_call(kernel, out_shape=jax.ShapeDtypeStruct(pair_act.shape, pai...]
where the time goes in v4:
time: 70.7 us; the launch traced here: 70.6 us
  Pallas kernels  68.9 us (97%)
  local copies, waits for them, and re-layouts  1.67 us (2%)
    pallas_call x1, Pallas kernels, shards(): pl.pallas_call(kernel, out_shape=jax.ShapeDtypeStruct(pair_act.shape, pai...  68.9 us
    unnamed x1, local copies, waits for them, and re-layouts  1.67 us

profile of v4, /device:TPU:1, one launch (start us, length us, event | category | flops | bytes accessed | tf_op | source)
XLA Modules:
  0.0 70.6 jit_solution(12475986606777755313)
XLA Ops:
  0.0 68.9 %shard_map.64 = bf16[32,32,128]{2,1,0:T(8,128)(2,1)} custom-call(s32[512]{0:T(512)} %mask_hbm.1, bf16[32,32,128]{2,1,0:T(8,128)(2,1)} %pair_hbm.1, bf16[128,640]{1,0:T(8,128)(2,1)} %w_out.1, bf16[128,128]{1,0:T(8,128)(2,1)} %f_out.1, bf16[128,640]{1,0:T(8,128)(2,1)} %w_in.1, bf16[128,128]{1,0:T(8,128)(2,1)} %f_in.1), custom_call_target="tpu_custom_call" | custom-call | tf_op jit(solution)/shard_map/pallas_call | solution.py:356
  68.9 1.7 %copy.8 = bf16[32,32,128]{2,1,0:T(8,128)(2,1)} copy(bf16[32,32,128]{2,1,0:T(8,128)(2,1)} %shard_map.64) | data formatting | bytes 524288

commit v5 on v4

--- a/solution.py
+++ b/solution.py
@@ -50,7 +50,7 @@
     pair_t, weights_t, final_t, half_mask, normed, mixed, gate, stage,
     send1, recv1, left, right_o, right_i, summed, send3, recv3,
     hidden, hidden_t,
-    s0, s1, r1, sf, rf, s3, r3, sx,
+    s0, s1, r1, sf, rf, s3, r3, sx, halves, sh, rh, fs, fr,
 ):
     loads = [
         pltpu.make_async_copy(src, dst, s0.at[i])
@@ -109,12 +109,31 @@
             src, dst, s1.at[u, d], r1.at[u, d // PER], {"row": row_to[d], "col": col_to[e]}
         )
 
+    def send_side(side, d, e):
+        src = send1.at[0, d, chip_to[e], side]
+        dst = halves.at[side, core, d // PER, d % PER, chip]
+        sem = rh.at[4 if side else d // PER]
+        if (d, e) == (SELF, 0):
+            pltpu.make_async_copy(src, dst, sem).start()
+        else:
+            to = {"row": row_to[d], "col": col_to[e]}
+            remote(src, dst, sh.at[side, d], sem, to).start()
+
+    def wait_side(side, g):
+        block = halves.at[1, core] if side else halves.at[0, core, g]
+        remote(block, block, sx, rh.at[4 if side else g], sibling).wait_recv()
+
+    def forward_side(side, g):
+        block = halves.at[1, core] if side else halves.at[0, core, g]
+        at = 4 if side else g
+        return remote(block, block, fs.at[at], fr.at[at], sibling)
+
     def wait1(u, g):
         block = recv1.at[u, core, g]
         remote(block, block, sx, r1.at[u, g], sibling).wait_recv()
 
     def forward1(u, g):
-        block = recv1.at[u, core, g] if u == 0 else recv1.at[u, core, g, :, :, 0]
+        block = recv1.at[u, core, g, :, :, 0]
         return remote(block, block, sf.at[u, g], rf.at[u, g], sibling)
 
     def send_sums(u, slot, to_row, e, own):
@@ -189,14 +208,9 @@
                 )
         return held[...].astype(jnp.bfloat16).reshape(8, 2, SUB, 128)
 
-    def turned_tiles(u, k, g, slots, v, side):
+    def turned_tiles(tile, slots, v):
         turned = block_transpose(
-            [
-                jnp.concatenate(
-                    [recv1[u, k, g, i, 4 * v + t, side] for i in slots], axis=0
-                )
-                for t in range(4)
-            ]
+            [jnp.concatenate([tile(i, 4 * v + t) for i in slots], axis=0) for t in range(4)]
         )
         return [
             jnp.concatenate([w[8 * i : 8 * i + 8] for w in turned], axis=0)
@@ -206,21 +220,41 @@
     def band(r):
         return pl.ds(pl.multiple_of(r * BLK, BLK), BLK)
 
-    def assemble(u, g, part):
-        k = core_at[part]
+    def assemble_left(g, part):
         for v in range(2):
             lanes = slice(256 * part + 128 * v, 256 * part + 128 * v + 128)
-            for i, rows in enumerate(turned_tiles(u, k, g, range(PER), v, 0)):
-                left[band(row_from[g * PER + i]), lanes] = rows
-            if u == 0:
-                step = (z + core + g) % 2
-                z_src = z_from[2 * g] + step * (z_from[2 * g + 1] - z_from[2 * g])
-                slots = [2 * step + a for a in range(2)]
-                for a, rows in enumerate(turned_tiles(u, k, g, slots, v, 1)):
-                    right_o[band(y_at[a] * 4 + z_src // 2), lanes] = rows
-            elif part == 0:
-                for i, rows in enumerate(turned_tiles(u, k, g, range(PER), v, 1)):
-                    right_i[band(row_from[g * PER + i]), lanes] = rows
+            tile = lambda i, p: halves[0, core_at[part], g, i, p]
+            for i, rows in enumerate(turned_tiles(tile, range(PER), v)):
+                left[(PER * g + i) * BLK : (PER * g + i + 1) * BLK, lanes] = rows
+
+    def assemble_right(g, part):
+        step = (z + core + g) % 2
+        z_src = z_from[2 * g] + step * (z_from[2 * g + 1] - z_from[2 * g])
+        for v in range(2):
+            lanes = slice(256 * part + 128 * v, 256 * part + 128 * v + 128)
+            tile = lambda i, p: halves[1, core_at[part], g, i, p]
+            for a, rows in enumerate(turned_tiles(tile, [2 * step + a for a in range(2)], v)):
+                right_o[band(y_at[a] * 4 + z_src // 2), lanes] = rows
+
+    def finish_rows(g):
+        forward_side(0, g).wait_recv()
+        assemble_left(g, 1)
+        rows = slice(128 * g, 128 * g + 128)
+        summed[rows, :] = lax.dot_general(
+            left[rows, :], right_o[...], (((1,), (1,)), ((), ())), preferred_element_type=jnp.float32
+        )
+        slots = range(PER * g, PER * g + PER)
+        turn_sums(0, slots, [d * BLK for d in slots])
+        for d, e in far_first(slots):
+            send_sums(0, d, row_from[d], e, True if (d, e) == (SELF, 0) else None)
+
+    def assemble(g, part):
+        for v in range(2):
+            lanes = slice(256 * part + 128 * v, 256 * part + 128 * v + 128)
+            for side in range(2 - part):
+                tile = lambda i, p: recv1[1, core_at[part], g, i, p, side]
+                for i, rows in enumerate(turned_tiles(tile, range(PER), v)):
+                    (left, right_i)[side][band(row_from[g * PER + i]), lanes] = rows
 
     def turn_sums(u, slots, at):
         for v in range(2):
@@ -243,14 +277,23 @@
     for u in range(2):
         project(u)
         if u == 0:
+            for d in range(ROWS):
+                send1[u, d] = sides(u, d)
             pl.semaphore_wait(barrier, 128)
 
+        if u == 0:
+            for d, e in far_first(range(ROWS)):
+                send_side(1, d, e)
         for g in range(CHUNKS):
             slots = range(g * PER, (g + 1) * PER)
-            for d in slots:
-                send1[u, d] = sides(u, d)
+            if u == 1:
+                for d in slots:
+                    send1[u, d] = sides(u, d)
             for d, e in far_first(slots):
-                copy1(u, d, e).start()
+                if u == 0:
+                    send_side(0, d, e)
+                else:
+                    copy1(u, d, e).start()
 
         gate[...] = 0.5 * jnp.tanh(0.5 * mixed[4 * CH :, :]) + 0.5
         if u == 0:
@@ -260,34 +303,32 @@
             for k in range(2):
                 final_t[k] = f_ref[k].astype(jnp.float32).T.astype(jnp.bfloat16)
 
-        for g in range(CHUNKS):
-            wait1(u, g)
-            forward1(u, g).start()
-            assemble(u, g, 0)
-
         if u == 0:
+            wait_side(1, 0)
+            forward_side(1, 0).start()
+            for g in range(CHUNKS):
+                assemble_right(g, 0)
+            for g in range(CHUNKS):
+                wait_side(0, g)
+                forward_side(0, g).start()
+                assemble_left(g, 0)
+                if g == 0:
+                    forward_side(1, 0).wait_recv()
+                    for k in range(CHUNKS):
+                        assemble_right(k, 1)
+                else:
+                    finish_rows(g - 1)
+            finish_rows(CHUNKS - 1)
+        else:
+            for g in range(CHUNKS):
+                wait1(u, g)
+                forward1(u, g).start()
+                assemble(g, 0)
             for part in range(2):
                 if part == 1:
                     for g in range(CHUNKS):
                         forward1(u, g).wait_recv()
-                        assemble(u, g, 1)
-                lanes = slice(256 * part, 256 * part + 256)
-                term = lax.dot_general(
-                    left[:, lanes], right_o[:, lanes], (((1,), (1,)), ((), ())),
-                    preferred_element_type=jnp.float32,
-                )
-                summed[...] = term if part == 0 else summed[...] + term
-            for g in range(4):
-                slots = range(4 * g, 4 * g + 4)
-                turn_sums(u, slots, [row_to[d] * BLK for d in slots])
-            for d, e in far_first(range(ROWS)):
-                send_sums(u, d, row_to[d], e, True if (d, e) == (SELF, 0) else None)
-        else:
-            for part in range(2):
-                if part == 1:
-                    for g in range(CHUNKS):
-                        forward1(u, g).wait_recv()
-                        assemble(u, g, 1)
+                        assemble(g, 1)
                 lanes = slice(256 * part, 256 * part + 256)
                 summed[lanes, :] = lax.dot_general(
                     left[:, lanes], right_i[...], (((0,), (0,)), ((), ())),
@@ -333,15 +374,18 @@
         for q in range(4):
             out_ref[8 * q + s] = block[32 * q : 32 * q + 32]
 
+    for d in range(ROWS):
+        count = 7 if d == SELF else 8
+        for side in range(2):
+            block = send1.at[0, d, pl.ds(0, count), side]
+            remote(block, block, sh.at[side, d], rh.at[0], sibling).wait_send()
+        block = send1.at[1, d, pl.ds(0, count)]
+        remote(block, block, s1.at[1, d], r1.at[1, 0], sibling).wait_send()
+    for g in range(CHUNKS):
+        forward_side(0, g).wait_send()
+        forward1(1, g).wait_send()
+    forward_side(1, 0).wait_send()
     for u in range(2):
-        for d in range(ROWS):
-            count = 7 if d == SELF else 8
-            remote(
-                send1.at[u, d, pl.ds(0, count)], send1.at[u, d, pl.ds(0, count)],
-                s1.at[u, d], r1.at[u, 0], sibling,
-            ).wait_send()
-        for g in range(CHUNKS):
-            forward1(u, g).wait_send()
         for slot in range(ROWS):
             count = 7 if slot in ((SELF,), (LAST, 8 + LAST))[u] else 8
             block = send3.at[u, slot, pl.ds(0, count)]
@@ -385,6 +429,8 @@
             dma((2, ROWS)), dma((2, CHUNKS)),
             dma((2, CHUNKS)), dma((2, CHUNKS)),
             dma((2, ROWS)), dma((2,)), dma,
+            pltpu.VMEM((2, 2, CHUNKS, PER, 8, SUB, 128), bf16),
+            dma((2, ROWS)), dma((5,)), dma((5,)), dma((5,)),
         ],
         compiler_params=pltpu.CompilerParams(
             collective_id=0, has_side_effects=True, vmem_limit_bytes=60 * 1024 * 1024

time: 70.7 us -> 70.1 us (level)
  no operation moved by 1% of the time
where the time goes in v5:
time: 70.1 us; the launch traced here: 69.9 us
  Pallas kernels  68.3 us (97%)
  local copies, waits for them, and re-layouts  1.67 us (2%)
    pallas_call x1, Pallas kernels, shards(): pl.pallas_call(kernel, out_shape=jax.ShapeDtypeStruct(pair_act.shape, pai...  68.3 us
    unnamed x1, local copies, waits for them, and re-layouts  1.67 us

profile of v5, /device:TPU:1, one launch (start us, length us, event | category | flops | bytes accessed | tf_op | source)
XLA Modules:
  0.0 69.9 jit_solution(10499879907528241750)
XLA Ops:
  0.0 68.3 %shard_map.64 = bf16[32,32,128]{2,1,0:T(8,128)(2,1)} custom-call(s32[512]{0:T(512)} %mask_hbm.1, bf16[32,32,128]{2,1,0:T(8,128)(2,1)} %pair_hbm.1, bf16[128,640]{1,0:T(8,128)(2,1)} %w_out.1, bf16[128,128]{1,0:T(8,128)(2,1)} %f_out.1, bf16[128,640]{1,0:T(8,128)(2,1)} %w_in.1, bf16[128,128]{1,0:T(8,128)(2,1)} %f_in.1), custom_call_target="tpu_custom_call" | custom-call | tf_op jit(solution)/shard_map/pallas_call | solution.py:400
  68.3 1.7 %copy.8 = bf16[32,32,128]{2,1,0:T(8,128)(2,1)} copy(bf16[32,32,128]{2,1,0:T(8,128)(2,1)} %shard_map.64) | data formatting | bytes 524288

commit v6 on v5

--- a/solution.py
+++ b/solution.py
@@ -284,15 +284,14 @@
         if u == 0:
             for d, e in far_first(range(ROWS)):
                 send_side(1, d, e)
-        for g in range(CHUNKS):
-            slots = range(g * PER, (g + 1) * PER)
-            if u == 1:
+            for g in range(CHUNKS):
+                for d, e in far_first(range(g * PER, (g + 1) * PER)):
+                    send_side(0, d, e)
+        else:
+            for slots in (range(1), range(1, 2), range(2, 4), range(4, 8), range(8, 16)):
                 for d in slots:
                     send1[u, d] = sides(u, d)
-            for d, e in far_first(slots):
-                if u == 0:
-                    send_side(0, d, e)
-                else:
+                for d, e in far_first(slots):
                     copy1(u, d, e).start()
 
         gate[...] = 0.5 * jnp.tanh(0.5 * mixed[4 * CH :, :]) + 0.5

time: 70.1 us -> 70 us (level)
  no operation moved by 1% of the time
where the time goes in v6:
time: 70 us; the launch traced here: 69.8 us
  Pallas kernels  68.2 us (97%)
  local copies, waits for them, and re-layouts  1.67 us (2%)
    pallas_call x1, Pallas kernels, shards(): pl.pallas_call(kernel, out_shape=jax.ShapeDtypeStruct(pair_act.shape, pai...  68.2 us
    unnamed x1, local copies, waits for them, and re-layouts  1.67 us

profile of v6, /device:TPU:1, one launch (start us, length us, event | category | flops | bytes accessed | tf_op | source)
XLA Modules:
  0.0 69.8 jit_solution(18127886543564625484)
XLA Ops:
  0.0 68.2 %shard_map.64 = bf16[32,32,128]{2,1,0:T(8,128)(2,1)} custom-call(s32[512]{0:T(512)} %mask_hbm.1, bf16[32,32,128]{2,1,0:T(8,128)(2,1)} %pair_hbm.1, bf16[128,640]{1,0:T(8,128)(2,1)} %w_out.1, bf16[128,128]{1,0:T(8,128)(2,1)} %f_out.1, bf16[128,640]{1,0:T(8,128)(2,1)} %w_in.1, bf16[128,128]{1,0:T(8,128)(2,1)} %f_in.1), custom_call_target="tpu_custom_call" | custom-call | tf_op jit(solution)/shard_map/pallas_call | solution.py:399
  68.2 1.7 %copy.8 = bf16[32,32,128]{2,1,0:T(8,128)(2,1)} copy(bf16[32,32,128]{2,1,0:T(8,128)(2,1)} %shard_map.64) | data formatting | bytes 524288
